TPU v7x, 32 devices: a whole 2x2x4 slice. The times are simulated.
32 devices in a mesh: groups: 2 (over y), ep: 16 (over z, x, core), tp: 1.
Axes of the slice: x: 2, y: 2, z: 4, core: 2. Of those that a mesh axis runs over, the one named last changes fastest.
Arguments:
- queries: bfloat16 [128, 32, 128], P(('groups', 'ep'), 'tp'), parts along dimension 0, may hold values from -6 to 6
- key_cache: bfloat16 [128, 128, 2, 128], P(('groups', 'ep'), None, 'tp'), parts along dimension 0, may hold values from -6 to 6
- value_cache: bfloat16 [128, 128, 2, 128], P(('groups', 'ep'), None, 'tp'), parts along dimension 0, may hold values from -6 to 6
- new_key: bfloat16 [128, 2, 128], P(('groups', 'ep'), 'tp'), parts along dimension 0, may hold values from -6 to 6
- new_value: bfloat16 [128, 2, 128], P(('groups', 'ep'), 'tp'), parts along dimension 0, may hold values from -6 to 6
- lengths: int32 [128], P(('groups', 'ep')), parts along dimension 0, may hold values from 1 to 128, as said below
- residual: bfloat16 [512, 2048], P(('groups', 'ep'), 'tp'), parts along dimension 0, may hold values from -6 to 6
- norm_gain: float32 [2048], replicated, may hold values from 0.5 to 1.5
- routes: int32 [512, 8], P(('groups', 'ep')), parts along dimension 0, may hold values from 0 to 15, all different within a row; in each aligned block of 16 rows (0 to 15, 16 to 31, ...) at most 16 rows name the same one
- route_weights: float32 [512, 8], P(('groups', 'ep')), parts along dimension 0, may hold values from 0.05 to 0.4
- expert_in: bfloat16 [16, 2, 2048, 768], P('ep', None, None, 'tp'), may hold values from -0.125 to 0.125
- expert_down: bfloat16 [16, 768, 2048], P('ep', 'tp'), may hold values from -0.21875 to 0.21875
Outputs:
- attended: bfloat16 [128, 32, 128], P(('groups', 'ep'), 'tp'), parts along dimension 0
- moe_out: bfloat16 [512, 2048], P(('groups', 'ep'), 'tp'), parts along dimension 0
There are 2 independent parts, one for each index of `groups`. A program takes and returns all parts, laid end to end along the dimension named above; an argument that names none is the same for every part. Nothing has to cross between parts.
Inputs may be any that keep to these rules, and one draw needn't show every extreme that they name: `routes`: each row names 8 different experts; among the 16 rows of one device (aligned blocks) no expert is named by more than 16 rows, a bound that some block reaches. `lengths`: the first row of every draw fills all 128 slots.
All inputs are finite; a program needn't handle non-finite values.
Results may differ from a plain program's by a relative error of at most 0.0075.
Values may be sent and summed in bfloat16 or wider, within the bound.
No kernel may reach another device: no remote copies, remote signals or barrier semaphores. Data moves between devices by JAX's collectives and lax.ppermute only.
A program may use at most 64 MiB of HBM per device.

v0:
```python
import jax
import jax.numpy as jnp
from jax import lax
from jax.sharding import PartitionSpec as P


def attention_block(queries, key_cache, value_cache, new_key, new_value, lengths):
    rows_here, heads_here, head_size = queries.shape
    kv_here = key_cache.shape[2]
    slots_here = key_cache.shape[1]
    group = heads_here // kv_here
    scale = 1.0 / head_size**0.5
    grouped = queries.reshape(rows_here, kv_here, group, head_size)
    scores = (
        jnp.einsum("akgd,ackd->akgc", grouped, key_cache, preferred_element_type=jnp.float32)
        * scale
    )
    valid = (jnp.arange(slots_here)[None, :] < lengths[:, None])[:, None, None, :]
    scores = jnp.where(valid, scores, -1e30)
    own_score = (
        jnp.einsum("akgd,akd->akg", grouped, new_key, preferred_element_type=jnp.float32) * scale
    )
    largest = jnp.maximum(jnp.max(scores, axis=-1), own_score)
    cache_exp = jnp.exp(scores - largest[..., None])
    own_exp = jnp.exp(own_score - largest)
    total = jnp.sum(cache_exp, axis=-1) + own_exp
    cache_probs = (cache_exp / total[..., None]).astype(jnp.bfloat16)
    own_probs = (own_exp / total).astype(jnp.bfloat16)
    mixed = jnp.einsum(
        "akgc,ackd->akgd", cache_probs, value_cache, preferred_element_type=jnp.float32
    )
    mixed = (
        mixed
        + own_probs.astype(jnp.float32)[..., None] * new_value.astype(jnp.float32)[:, :, None, :]
    )
    return mixed.reshape(rows_here, heads_here, head_size).astype(jnp.bfloat16)


def per_device(
    queries,
    key_cache,
    value_cache,
    new_key,
    new_value,
    lengths,
    residual,
    norm_gain,
    routes,
    route_weights,
    expert_in,
    expert_down,
):
    attended = attention_block(queries, key_cache, value_cache, new_key, new_value, lengths)
    row_count, top_count = routes.shape
    expert_count = expert_in.shape[0] * lax.axis_size("ep")
    capacity = min(row_count, max(2, 2 * row_count * top_count // expert_count))
    whole = lax.all_gather(residual, "tp", axis=1, tiled=True)
    width = whole.shape[1]
    half_width = residual.shape[1]
    wide = whole.astype(jnp.float32)
    normed = (
        wide * lax.rsqrt(jnp.mean(wide * wide, axis=1, keepdims=True) + 1e-06) * norm_gain
    ).astype(jnp.bfloat16)
    flat_routes = routes.reshape(-1)
    hits = (flat_routes[:, None] == jnp.arange(expert_count)[None, :]).astype(jnp.int32)
    before = jnp.cumsum(hits, axis=0) - hits
    position = jnp.sum(before * hits, axis=1)
    slot_flat = flat_routes * capacity + position
    placed = (slot_flat[:, None] == jnp.arange(expert_count * capacity)[None, :]).astype(
        jnp.float32
    )
    placed = placed.reshape(row_count, top_count, expert_count * capacity)
    selector = jnp.sum(placed, axis=1).astype(jnp.bfloat16)
    buffer = jnp.einsum("rs,rd->sd", selector, normed, preferred_element_type=jnp.float32)
    buffer = buffer.astype(jnp.bfloat16).reshape(expert_count, capacity, width)
    arrived = lax.all_to_all(buffer, "ep", split_axis=0, concat_axis=0, tiled=True)
    sources = arrived.shape[0]
    flat_rows = arrived.reshape(sources * capacity, width)
    gate_act = jnp.dot(flat_rows, expert_in[0, 0], preferred_element_type=jnp.float32)
    up_act = jnp.dot(flat_rows, expert_in[0, 1], preferred_element_type=jnp.float32)
    hidden = (jax.nn.silu(gate_act) * up_act).astype(jnp.bfloat16)
    partial_value = jnp.dot(hidden, expert_down[0], preferred_element_type=jnp.float32)
    partial_value = partial_value.reshape(sources, capacity, width)
    summed = lax.psum_scatter(partial_value, "tp", scatter_dimension=2, tiled=True).astype(
        jnp.bfloat16
    )
    returned = lax.all_to_all(summed, "ep", split_axis=0, concat_axis=0, tiled=True)
    weighting = jnp.sum(placed * route_weights[:, :, None], axis=1)
    gathered_rows = returned.reshape(expert_count * capacity, half_width).astype(jnp.float32)
    combined = jnp.dot(weighting, gathered_rows, precision=lax.Precision.HIGHEST)
    moe_out = (residual.astype(jnp.float32) + combined).astype(jnp.bfloat16)
    return (attended, moe_out)


def solution(mesh):
    in_specs = (
        P(("groups", "ep"), "tp", None),
        P(("groups", "ep"), None, "tp", None),
        P(("groups", "ep"), None, "tp", None),
        P(("groups", "ep"), "tp", None),
        P(("groups", "ep"), "tp", None),
        P(("groups", "ep")),
        P(("groups", "ep"), "tp"),
        P(),
        P(("groups", "ep"), None),
        P(("groups", "ep"), None),
        P("ep", None, None, "tp"),
        P("ep", "tp", None),
    )
    out_specs = (P(("groups", "ep"), "tp", None), P(("groups", "ep"), "tp"))
    return jax.shard_map(
        per_device, mesh=mesh, in_specs=in_specs, out_specs=out_specs, check_vma=False
    )
```

profile of v0, /device:TPU:0, one launch (start us, length us, event | category | flops | bytes accessed | tf_op | source)
XLA Modules:
  0.0 74.7 jit_solution(11768580950044539288)
XLA Ops:
  0.6 0.0 copy-start
  0.6 1.1 %fusion.22 = f32[16]{0:T(128)S(1)} fusion(bf16[16,2048]{1,0:T(8,128)(2,1)} %param.18), kind=kLoop, calls=%fused_computation.22 | loop fusion | flops 98288 | bytes 65600 | tf_op jit(solution)/shard_map/reduce_sum | solution.py:62
  1.8 0.8 %copy.26 = s32[16,8]{1,0:T(8,128)S(1)} copy(s32[16,8]{0,1:T(8,128)} %param.20) | data formatting | bytes 1024 | tf_op args[8]
  2.5 0.1 eq.29
  2.6 0.8 %copy.28 = f32[16,8]{1,0:T(8,128)S(1)} copy(f32[16,8]{0,1:T(8,128)} %param.21) | data formatting | bytes 1024 | tf_op args[9]
  3.4 0.1 fusion.28
  3.5 0.2 reduce_window_sum.11
  3.6 0.2 select_reduce_fusion.1
  3.8 0.1 reduce_sum.49
  3.9 0.2 convert_reduce_fusion
  4.1 1.3 %convolution_convert_fusion = bf16[256,2048]{1,0:T(8,128)(2,1)S(1)} fusion(bf16[16,2048]{1,0:T(8,128)(2,1)} %param.18, f32[2048]{0:T(1024)} %param.19, f32[16]{0:T(128)S(1)} %add_rsqrt_fusion, bf16[16,256]{1,0:T(8,128)(2,1)S(1)} %get-tuple-element.2), kind=kOutput, calls=%fused_computation.9 | convolution fusion | flops 17432576 | bytes 1130560 | tf_op jit(solution)/shard_map/rs,rd->sd/dot_general | solution.py:74
  5.4 32.0 %all_to_all.10 = bf16[16,16,2048]{2,1,0:T(8,128)(2,1)S(1)} all-to-all(bf16[16,16,2048]{2,1,0:T(8,128)(2,1)S(1)} %bitcast.33), channel_id=1, replica_groups=mesh['groups'=2,'ep'=16,'tp'=1] {'ep'}, dimensions={0} | all-to-all | bytes 2097152 | tf_op jit(solution)/shard_map/all_to_all | solution.py:76
  37.4 0.0 copy-start.5
  37.4 3.0 %fusion.4 = f32[256,768]{1,0:T(8,128)S(1)} fusion(bf16[256,2048]{1,0:T(8,128)(2,1)S(1)} %bitcast.34, bf16[1,2,2048,768]{3,2,1,0:T(8,128)(2,1)} %param.22), kind=kOutput, calls=%fused_computation.4 | convolution fusion | flops 805306368 | bytes 4980736 | tf_op jit(solution)/shard_map/dot_general | solution.py:79
  40.5 0.7 copy-done.5
  41.1 1.0 %fusion.15 = bf16[256,768]{1,0:T(8,128)(2,1)S(1)} fusion(bf16[256,2048]{1,0:T(8,128)(2,1)S(1)} %bitcast.35, bf16[1,2,2048,768]{3,2,1,0:T(8,128)(2,1)S(1)} %copy-done.5, f32[256,768]{1,0:T(8,128)S(1)} %fusion.4), kind=kOutput, calls=%fused_computation.13 | convolution fusion | flops 806486016 | bytes 5373952 | tf_op jit(solution)/shard_map/dot_general | solution.py:80
  42.2 0.0 copy-done
  42.2 0.0 copy-start.4
  42.2 0.0 copy-start.7
  42.2 0.0 copy-start.3
  42.2 0.0 copy-start.6
  42.2 0.0 copy-start.2
  42.2 0.0 copy-start.1
  42.2 2.1 %fusion.8 = bf16[16,16,2048]{2,1,0:T(8,128)(2,1)} fusion(bf16[16,16,768]{2,1,0:T(8,128)(2,1)S(1)} %bitcast.41, bf16[1,768,2048]{2,1,0:T(8,128)(2,1)S(1)} %copy-done), kind=kOutput, calls=%fused_computation.8 | convolution fusion | flops 805830656 | bytes 4587520 | tf_op jit(solution)/shard_map/dot_general | solution.py:82
  44.3 5.0 %all-to-all-start.1 = ((bf16[16,16,2048]{2,1,0:T(8,128)(2,1)}), bf16[16,16,2048]{2,1,0:T(8,128)(2,1)}, u32[]{:S(2)}, u32[]{:S(2)}) async-start(bf16[16,16,2048]{2,1,0:T(8,128)(2,1)} %fusion.8), calls=%async_computation.1 | async-start | bytes 2097152 | tf_op jit(solution)/shard_map/all_to_all | solution.py:87
  49.4 0.0 copy-done.4
  49.4 0.0 copy-done.7
  49.4 0.1 iota_compare_fusion.2
  49.5 0.0 copy-done.3
  49.5 0.0 copy-done.6
  49.5 0.1 fusion.33
  49.6 0.0 copy-done.2
  49.6 0.3 fusion.37
  50.0 0.2 fusion.29
  50.2 1.8 %fusion.19 = bf16[4,2,16,128]{3,2,1,0:T(8,128)(2,1)} fusion(bf16[4,128,2,128]{3,2,1,0:T(2,128)(2,1)} %param.14, f32[4,2,16,128]{3,2,1,0:T(8,128)S(1)} %get-tuple-element.7, f32[4,2,128]{2,1,0:T(2,128)S(1)} %convert_element_type.51, f32[4,2,16]{2,1,0:T(2,128)S(1)} %get-tuple-element.5, f32[4,2,16]{2,1,0:T(2,128)S(1)} %get-tuple-element.4, ...), kind=kOutput, calls=%fused_computation.17 | convolution fusion | flops 4292608 | bytes 366080 | tf_op jit(solution)/shard_map/akgc,ackd->akgd/dot_general | solution.py:29
  52.0 20.4 %all-to-all-done.1 = bf16[16,16,2048]{2,1,0:T(8,128)(2,1)} async-done(((bf16[16,16,2048]{2,1,0:T(8,128)(2,1)}), bf16[16,16,2048]{2,1,0:T(8,128)(2,1)}, u32[]{:S(2)}, u32[]{:S(2)}) %all-to-all-start.1) | async-done | bytes 1048608 | tf_op jit(solution)/shard_map/all_to_all | solution.py:87
  72.4 0.0 copy-done.1
  72.4 2.4 %fusion.11 = bf16[16,2048]{1,0:T(8,128)(2,1)} fusion(f32[16,256]{1,0:T(8,128)S(1)} %get-tuple-element.3, bf16[256,2048]{1,0:T(8,128)(2,1)} %bitcast.12, bf16[16,2048]{1,0:T(8,128)(2,1)S(1)} %copy-done.1), kind=kOutput, calls=%fused_computation.11 | convolution fusion | flops 100761600 | bytes 1196032 | tf_op jit(solution)/shard_map/dot_general | solution.py:90
  (5 shorter events, 0.1 us)
Async XLA Ops:
  0.6 41.5 %copy-start = (bf16[1,768,2048]{2,1,0:T(8,128)(2,1)S(1)}, bf16[1,768,2048]{2,1,0:T(8,128)(2,1)}, u32[]{:S(2)}) copy-start(bf16[1,768,2048]{2,1,0:T(8,128)(2,1)} %param.23) | copy-start | bytes 9437188
  37.4 3.7 %copy-start.5 = (bf16[1,2,2048,768]{3,2,1,0:T(8,128)(2,1)S(1)}, bf16[1,2,2048,768]{3,2,1,0:T(8,128)(2,1)}, u32[]{:S(2)}) copy-start(bf16[1,2,2048,768]{3,2,1,0:T(8,128)(2,1)} %param.22) | copy-start | bytes 18874372
  42.2 7.2 %copy-start.4 = (bf16[4,2,128]{2,1,0:T(2,128)(2,1)S(1)}, bf16[4,2,128]{2,1,0:T(2,128)(2,1)}, u32[]{:S(2)}) copy-start(bf16[4,2,128]{2,1,0:T(2,128)(2,1)} %param.16) | copy-start | bytes 6148
  42.2 7.2 %copy-start.7 = (s32[4]{0:T(128)S(1)}, s32[4]{0:T(128)}, u32[]{:S(2)}) copy-start(s32[4]{0:T(128)} %param.17) | copy-start | bytes 52
  42.2 7.3 %copy-start.3 = (bf16[4,32,128]{2,1,0:T(8,128)(2,1)S(1)}, bf16[4,32,128]{2,1,0:T(8,128)(2,1)}, u32[]{:S(2)}) copy-start(bf16[4,32,128]{2,1,0:T(8,128)(2,1)} %param.12) | copy-start | bytes 98308
  42.2 7.3 %copy-start.6 = (bf16[4,2,128]{2,1,0:T(2,128)(2,1)S(1)}, bf16[4,2,128]{2,1,0:T(2,128)(2,1)}, u32[]{:S(2)}) copy-start(bf16[4,2,128]{2,1,0:T(2,128)(2,1)} %param.15) | copy-start | bytes 6148
  42.2 7.4 %copy-start.2 = (bf16[4,128,2,128]{3,2,1,0:T(2,128)(2,1)S(1)}, bf16[4,128,2,128]{3,2,1,0:T(2,128)(2,1)}, u32[]{:S(2)}) copy-start(bf16[4,128,2,128]{3,2,1,0:T(2,128)(2,1)} %param.13) | copy-start | bytes 786436
  42.2 30.1 %copy-start.1 = (bf16[16,2048]{1,0:T(8,128)(2,1)S(1)}, bf16[16,2048]{1,0:T(8,128)(2,1)}, u32[]{:S(2)}) copy-start(bf16[16,2048]{1,0:T(8,128)(2,1)} %param.18) | copy-start | bytes 196612
  44.3 28.0 %all-to-all-start.1 = ((bf16[16,16,2048]{2,1,0:T(8,128)(2,1)}), bf16[16,16,2048]{2,1,0:T(8,128)(2,1)}, u32[]{:S(2)}, u32[]{:S(2)}) async-start(bf16[16,16,2048]{2,1,0:T(8,128)(2,1)} %fusion.8), calls=%async_computation.1 | async-start | bytes 2097152 | tf_op jit(solution)/shard_map/all_to_all | solution.py:87
where the time goes:
time: 76.2 us; the launch traced here: 74.7 us
  blocking collectives  32 us (42%)
  waiting for transfers between devices  20.4 us (27%)
  matrix products  12.1 us (16%)
  starting transfers between devices  5.04 us (7%)
  local copies, waits for them, and re-layouts  2.43 us (3%)
  other arithmetic  2.02 us (3%)
  between operations  0.8 us (1%)
    all_to_all x1, blocking collectives, per_device(): lax.all_to_all(buffer, 'ep', split_axis=0, concat_axis=0, tiled=True)  32 us
    all_to_all x1, waiting for transfers between devices, per_device(): lax.all_to_all(summed, 'ep', split_axis=0, concat_axis=0, tiled=True)  20.4 us
    all_to_all x1, starting transfers between devices, per_device(): lax.all_to_all(summed, 'ep', split_axis=0, concat_axis=0, tiled=True)  5.04 us
    dot_general x1, matrix products, per_device(): jnp.dot(flat_rows, expert_in[0, 0], preferred_element_type=jnp.float32)  3.03 us
    dot_general x1, matrix products, per_device(): jnp.dot(weighting, gathered_rows, precision=lax.Precision.HIGHEST)  2.38 us
    unnamed x18, local copies, waits for them, and re-layouts  2.26 us
    dot_general x1, matrix products, per_device(): jnp.dot(hidden, expert_down[0], preferred_element_type=jnp.float32)  2.06 us
    dot_general x1, matrix products, attention_block(): jnp.einsum('akgc,ackd->akgd', cache_probs, value_cache, preferred_element...  1.82 us
  transfers between devices with their start and end apart: 1, of which 1 were waited for; matrix products, arithmetic and copies ran while one was open for 3% of the time, Pallas kernels for 0%

commit v1 on v0

--- a/solution.py
+++ b/solution.py
@@ -36,31 +36,46 @@
     return mixed.reshape(rows_here, heads_here, head_size).astype(jnp.bfloat16)
 
 
-def per_device(
-    queries,
-    key_cache,
-    value_cache,
-    new_key,
-    new_value,
-    lengths,
-    residual,
-    norm_gain,
-    routes,
-    route_weights,
-    expert_in,
-    expert_down,
-):
-    attended = attention_block(queries, key_cache, value_cache, new_key, new_value, lengths)
+def normalize(residual, norm_gain):
+    wide = residual.astype(jnp.float32)
+    return (
+        wide * lax.rsqrt(jnp.mean(wide * wide, axis=1, keepdims=True) + 1e-06) * norm_gain
+    ).astype(jnp.bfloat16)
+
+
+def expert_layer_gathered(residual, norm_gain, routes, route_weights, expert_in, expert_down):
+    row_count, width = residual.shape
+    expert_count = lax.axis_size("ep")
+    normed = normalize(residual, norm_gain)
+    named = routes[:, :, None] == jnp.arange(expert_count)[None, None, :]
+    weight = jnp.sum(jnp.where(named, route_weights[:, :, None], 0.0), axis=1)
+    high = weight.astype(jnp.bfloat16)
+    low = (weight - high.astype(jnp.float32)).astype(jnp.bfloat16)
+    pad = jnp.zeros((row_count, 128 - 2 * expert_count % 128), jnp.bfloat16)
+    packed = jnp.concatenate([normed, high, low, pad], axis=1)
+    everyone = lax.all_gather(packed, "ep", axis=0, tiled=True)
+    rows = everyone[:, :width]
+    me = lax.axis_index("ep")
+    pieces = everyone[:, width : width + 2 * expert_count].astype(jnp.float32)
+    pieces = pieces.reshape(-1, 2, expert_count)
+    mine = jnp.sum(jnp.where(jnp.arange(expert_count) == me, pieces, 0.0), axis=(1, 2))
+    gate_act = jnp.dot(rows, expert_in[0, 0], preferred_element_type=jnp.float32)
+    up_act = jnp.dot(rows, expert_in[0, 1], preferred_element_type=jnp.float32)
+    hidden = (jax.nn.silu(gate_act) * up_act).astype(jnp.bfloat16)
+    out = jnp.dot(hidden, expert_down[0], preferred_element_type=jnp.float32)
+    weighted = (out * mine[:, None]).astype(jnp.bfloat16)
+    combined = lax.psum_scatter(weighted, "ep", scatter_dimension=0, tiled=True)
+    return (residual.astype(jnp.float32) + combined.astype(jnp.float32)).astype(jnp.bfloat16)
+
+
+def expert_layer_routed(residual, norm_gain, routes, route_weights, expert_in, expert_down):
     row_count, top_count = routes.shape
     expert_count = expert_in.shape[0] * lax.axis_size("ep")
     capacity = min(row_count, max(2, 2 * row_count * top_count // expert_count))
     whole = lax.all_gather(residual, "tp", axis=1, tiled=True)
     width = whole.shape[1]
     half_width = residual.shape[1]
-    wide = whole.astype(jnp.float32)
-    normed = (
-        wide * lax.rsqrt(jnp.mean(wide * wide, axis=1, keepdims=True) + 1e-06) * norm_gain
-    ).astype(jnp.bfloat16)
+    normed = normalize(whole, norm_gain)
     flat_routes = routes.reshape(-1)
     hits = (flat_routes[:, None] == jnp.arange(expert_count)[None, :]).astype(jnp.int32)
     before = jnp.cumsum(hits, axis=0) - hits
@@ -88,7 +103,27 @@
     weighting = jnp.sum(placed * route_weights[:, :, None], axis=1)
     gathered_rows = returned.reshape(expert_count * capacity, half_width).astype(jnp.float32)
     combined = jnp.dot(weighting, gathered_rows, precision=lax.Precision.HIGHEST)
-    moe_out = (residual.astype(jnp.float32) + combined).astype(jnp.bfloat16)
+    return (residual.astype(jnp.float32) + combined).astype(jnp.bfloat16)
+
+
+def per_device(
+    queries,
+    key_cache,
+    value_cache,
+    new_key,
+    new_value,
+    lengths,
+    residual,
+    norm_gain,
+    routes,
+    route_weights,
+    expert_in,
+    expert_down,
+):
+    attended = attention_block(queries, key_cache, value_cache, new_key, new_value, lengths)
+    dense = lax.axis_size("tp") == 1 and lax.axis_size("ep") <= 4 * routes.shape[1]
+    expert_layer = expert_layer_gathered if dense else expert_layer_routed
+    moe_out = expert_layer(residual, norm_gain, routes, route_weights, expert_in, expert_down)
     return (attended, moe_out)
 
 

time: 76.2 us -> 129 us (1.69)
  waiting for transfers between devices: 20.4 us -> 94.7 us
  blocking collectives: 32 us -> 0 us
  between operations: 0.8 us -> 14.2 us
  starting transfers between devices: 5.04 us -> 0.08 us
  other arithmetic: 2.02 us -> 4.9 us
    reduce_scatter x0 -> x1, waiting for transfers between devices: none -> 53.9 us  [expert_layer_gathered(): combined = lax.psum_scatter(weighted, 'ep', scatter_dimension=0, tiled=True)]
    all_gather x0 -> x1, waiting for transfers between devices: none -> 40.8 us  [expert_layer_gathered(): everyone = lax.all_gather(packed, 'ep', axis=0, tiled=True)]
    all_to_all x1 -> x0, blocking collectives: 32 us -> none  [per_device(): lax.all_to_all(buffer, 'ep', split_axis=0, concat_axis=0, tiled=True)]
    all_to_all x1 -> x0, waiting for transfers between devices: 20.4 us -> none  [per_device(): lax.all_to_all(summed, 'ep', split_axis=0, concat_axis=0, tiled=True)]
    all_to_all x1 -> x0, starting transfers between devices: 5.04 us -> none  [per_device(): lax.all_to_all(summed, 'ep', split_axis=0, concat_axis=0, tiled=True)]
    convert_element_type x1 -> x3, other arithmetic: 0.08 us -> 2.42 us  [the longest x1 1.49 us: expert_layer_gathered(): (residual.astype(jnp.float32) + combined.astype(jnp.float32)).astype(jnp....]
    dot_general x5 -> x2, matrix products: 9.81 us -> 9.69 us  [the longest x1 5.59 us: expert_layer_gathered(): out = jnp.dot(hidden, expert_down[0], preferred_element_type=jnp.float32)]
  transfers between devices with their start and end apart: 1 -> 2, of which waited for: 1 -> 2; matrix products, arithmetic and copies ran while one was open for 3% -> 2% of each run, Pallas kernels for 0% -> 0%
where the time goes in v1:
time: 129 us; the launch traced here: 128 us
  waiting for transfers between devices  94.7 us (73%)
  between operations  14.2 us (11%)
  matrix products  12 us (9%)
  other arithmetic  4.9 us (4%)
  local copies, waits for them, and re-layouts  2.37 us (2%)
    reduce_scatter x1, waiting for transfers between devices, expert_layer_gathered(): combined = lax.psum_scatter(weighted, 'ep', scatter_dimension=0, tiled=True)  53.9 us
    all_gather x1, waiting for transfers between devices, expert_layer_gathered(): everyone = lax.all_gather(packed, 'ep', axis=0, tiled=True)  40.8 us
    dot_general x1, matrix products, expert_layer_gathered(): out = jnp.dot(hidden, expert_down[0], preferred_element_type=jnp.float32)  5.59 us
    dot_general x1, matrix products, expert_layer_gathered(): jnp.dot(rows, expert_in[0, 0], preferred_element_type=jnp.float32)  4.1 us
  transfers between devices with their start and end apart: 2, of which 2 were waited for; matrix products, arithmetic and copies ran while one was open for 2% of the time, Pallas kernels for 0%

profile of v1, /device:TPU:0, one launch (start us, length us, event | category | flops | bytes accessed | tf_op | source)
XLA Modules:
  0.0 128.2 jit_solution(16159815102711095985)
XLA Ops:
  7.2 0.0 copy-start
  7.2 0.0 all-gather.2.cloned.1.call-start
  7.2 1.1 fusion.31
  8.4 0.8 copy.20
  9.1 0.8 copy.21
  9.9 0.1 select_reduce_fusion.1
  10.0 0.9 fusion.33
  10.9 0.7 concatenate.3
  11.7 0.0 all-gather.2.cloned.1.call-update
  11.7 0.0 reduce-scatter.2.cloned.1.call-start
  11.8 0.1 broadcast_in_dim.58
  11.8 40.8 %all-gather.2.cloned.1.call-done = bf16[256,2176]{1,0:T(8,128)(2,1)} async-done(((bf16[16,2176]{1,0:T(8,128)(2,1)}), bf16[256,2176]{1,0:T(8,128)(2,1)}) %all-gather.2.cloned.1.call-update) | async-done | bytes 1114128 | tf_op jit(solution)/shard_map/all_gather | solution.py:56
  52.7 0.9 select_reduce_fusion
  53.6 4.1 %fusion.4 = f32[256,768]{1,0:T(8,128)} fusion(bf16[1,2,2048,768]{3,2,1,0:T(8,128)(2,1)} %param.22, bf16[256,2176]{1,0:T(8,128)(2,1)} %all-gather.2.cloned.1.call-done), kind=kOutput, calls=%fused_computation.4 | convolution fusion | flops 805306368 | bytes 4980736 | tf_op jit(solution)/shard_map/dot_general | solution.py:62
  57.7 0.0 copy-done
  57.7 0.0 copy-start.4
  57.7 0.0 copy-start.6
  57.7 0.0 copy-start.3
  57.8 0.0 copy-start.5
  57.8 0.0 copy-start.2
  57.8 0.0 copy-start.1
  57.8 5.6 %fusion.11 = bf16[256,2048]{1,0:T(8,128)(2,1)} fusion(bf16[1,768,2048]{2,1,0:T(8,128)(2,1)S(1)} %copy-done, f32[256]{0:T(256)S(1)} %select_reduce_fusion, bf16[1,2,2048,768]{3,2,1,0:T(8,128)(2,1)} %param.22, bf16[256,2176]{1,0:T(8,128)(2,1)} %all-gather.2.cloned.1.call-done, f32[256,768]{1,0:T(8,128)} %fusion.4), kind=kOutput, calls=%fused_computation.9 | convolution fusion | flops 1612840960 | bytes 9176064 | tf_op jit(solution)/shard_map/dot_general | solution.py:65
  63.4 0.0 reduce-scatter.2.cloned.1.call-update
  63.4 0.0 copy-done.4
  63.4 0.0 copy-done.6
  63.4 0.1 iota_compare_fusion.1
  63.5 0.0 copy-done.3
  63.5 0.0 copy-done.5
  63.5 0.1 fusion.38
  63.6 0.0 copy-done.2
  63.6 0.3 fusion.43
  64.0 0.2 fusion.35
  64.2 1.8 %fusion.21 = bf16[4,2,16,128]{3,2,1,0:T(8,128)(2,1)} fusion(bf16[4,128,2,128]{3,2,1,0:T(2,128)(2,1)} %param.14, f32[4,2,16,128]{3,2,1,0:T(8,128)S(1)} %get-tuple-element.7, f32[4,2,128]{2,1,0:T(2,128)S(1)} %convert_element_type.52, f32[4,2,16]{2,1,0:T(2,128)S(1)} %get-tuple-element.5, f32[4,2,16]{2,1,0:T(2,128)S(1)} %get-tuple-element.4, ...), kind=kOutput, calls=%fused_computation.15 | convolution fusion | flops 4292608 | bytes 366080 | tf_op jit(solution)/shard_map/akgc,ackd->akgd/dot_general | solution.py:29
  66.0 53.9 %reduce-scatter.2.cloned.1.call-done = bf16[16,2048]{1,0:T(8,128)(2,1)} async-done(((bf16[256,2048]{1,0:T(8,128)(2,1)}), bf16[16,2048]{1,0:T(8,128)(2,1)}) %reduce-scatter.2.cloned.1.call-update) | async-done | bytes 65552 | tf_op jit(solution)/shard_map/reduce_scatter | solution.py:67
  119.9 0.0 copy-done.1
  119.9 1.5 %fusion.34 = bf16[16,2048]{1,0:T(8,128)(2,1)} fusion(bf16[16,2048]{1,0:T(8,128)(2,1)S(1)} %copy-done.1, bf16[16,2048]{1,0:T(8,128)(2,1)} %reduce-scatter.2.cloned.1.call-done), kind=kLoop, calls=%fused_computation.27 | loop fusion | flops 131072 | bytes 196608 | tf_op jit(solution)/shard_map/convert_element_type | solution.py:68
  (8 shorter events, 0.1 us)
Async XLA Ops:
  7.2 50.6 %copy-start = (bf16[1,768,2048]{2,1,0:T(8,128)(2,1)S(1)}, bf16[1,768,2048]{2,1,0:T(8,128)(2,1)}, u32[]{:S(2)}) copy-start(bf16[1,768,2048]{2,1,0:T(8,128)(2,1)} %param.23) | copy-start | bytes 9437188
  7.2 45.5 %all-gather.2.cloned.1.call-start = ((), (), s32[]{:S(2)}) async-start(), calls=%async_computation.1 | async-start | bytes 1183744 | tf_op jit(solution)/shard_map/all_gather | solution.py:56
  11.7 108.2 %reduce-scatter.2.cloned.1.call-start = ((), (), s32[]{:S(2)}) async-start(), calls=%async_computation.2 | async-start | bytes 1114112 | tf_op jit(solution)/shard_map/reduce_scatter | solution.py:67
  57.7 5.7 %copy-start.4 = (bf16[4,2,128]{2,1,0:T(2,128)(2,1)S(1)}, bf16[4,2,128]{2,1,0:T(2,128)(2,1)}, u32[]{:S(2)}) copy-start(bf16[4,2,128]{2,1,0:T(2,128)(2,1)} %param.16) | copy-start | bytes 6148
  57.7 5.7 %copy-start.6 = (s32[4]{0:T(128)S(1)}, s32[4]{0:T(128)}, u32[]{:S(2)}) copy-start(s32[4]{0:T(128)} %param.17) | copy-start | bytes 52
  57.7 5.8 %copy-start.3 = (bf16[4,32,128]{2,1,0:T(8,128)(2,1)S(1)}, bf16[4,32,128]{2,1,0:T(8,128)(2,1)}, u32[]{:S(2)}) copy-start(bf16[4,32,128]{2,1,0:T(8,128)(2,1)} %param.12) | copy-start | bytes 98308
  57.8 5.8 %copy-start.5 = (bf16[4,2,128]{2,1,0:T(2,128)(2,1)S(1)}, bf16[4,2,128]{2,1,0:T(2,128)(2,1)}, u32[]{:S(2)}) copy-start(bf16[4,2,128]{2,1,0:T(2,128)(2,1)} %param.15) | copy-start | bytes 6148
  57.8 5.9 %copy-start.2 = (bf16[4,128,2,128]{3,2,1,0:T(2,128)(2,1)S(1)}, bf16[4,128,2,128]{3,2,1,0:T(2,128)(2,1)}, u32[]{:S(2)}) copy-start(bf16[4,128,2,128]{3,2,1,0:T(2,128)(2,1)} %param.13) | copy-start | bytes 786436
  57.8 62.1 %copy-start.1 = (bf16[16,2048]{1,0:T(8,128)(2,1)S(1)}, bf16[16,2048]{1,0:T(8,128)(2,1)}, u32[]{:S(2)}) copy-start(bf16[16,2048]{1,0:T(8,128)(2,1)} %param.18) | copy-start | bytes 196612
Sparse Core Ops, SparseCore 0:
  11.8 40.8 all-gather.1
  63.5 56.3 reduce-scatter.1
